TPU v7x, 32 devices: a whole 2x2x4 slice. The times are simulated.
32 devices in a mesh: parts: 2 (over y), ctx: 4 (over z), chan: 2 (over x), sub: 2 (over core).
Axes of the slice: x: 2, y: 2, z: 4, core: 2. Of those that a mesh axis runs over, the one named last changes fastest.
Arguments:
- query_rows: bfloat16 [1024, 8192], P(('parts', 'ctx'), ('chan', 'sub')), parts along dimension 0, may hold values from -6 to 6
- key_rows: bfloat16 [1024, 8192], P(('parts', 'ctx'), ('chan', 'sub')), parts along dimension 0, may hold values from -6 to 6
- value_rows: bfloat16 [1024, 8192], P(('parts', 'ctx'), ('chan', 'sub')), parts along dimension 0, may hold values from -6 to 6
- short_filter: float32 [3, 3, 8192], P(None, None, ('chan', 'sub')), may hold values from -3.5 to 3.5
- decay_rate: float32 [16, 8192], P(None, ('chan', 'sub')), may hold values from 9.765625e-05 to 0.05
- residue: float32 [16, 8192], P(None, ('chan', 'sub')), may hold values from -3 to 3
- bypass: float32 [8192], P(('chan', 'sub')), may hold values from -4 to 4
Outputs:
- mixed_out: bfloat16 [1024, 8192], P(('parts', 'ctx'), ('chan', 'sub')), parts along dimension 0
There are 2 independent parts, one for each index of `parts`. A program takes and returns all parts, laid end to end along the dimension named above; an argument that names none is the same for every part. Nothing has to cross between parts.
All inputs are finite; a program needn't handle non-finite values.
Results may differ from a plain program's by a relative error of at most 0.001.
Values may be sent and summed in bfloat16 or wider, within the bound.
A program may use at most 128 MiB of HBM per device.

v0:
```python
import jax
import jax.numpy as jnp
from jax import lax
from jax.sharding import PartitionSpec as P

HIGH = lax.Precision.HIGHEST


def shifted(value, axis, steps):
    count = lax.axis_size(axis)
    leading, last = (max(0, -steps), min(count, count - steps))
    return lax.ppermute(value, axis, [(source, source + steps) for source in range(leading, last)])


def featurize(signal, taps, previous):
    joined = jnp.concatenate([previous, signal], axis=0).astype(jnp.float32)
    length = signal.shape[0]
    return taps[0] * joined[2:] + taps[1] * joined[1 : length + 1] + taps[2] * joined[0:length]


def combine(earlier, later):
    return (earlier[0] * later[0], later[0] * earlier[1] + later[1])


def block_tables(decay_rate, residue, block_len):
    offsets = jnp.arange(block_len).astype(jnp.float32)
    mode_gain = jnp.sqrt(-jnp.expm1(-2.0 * decay_rate))
    powers = jnp.exp(-decay_rate[:, None, :] * offsets[None, :, None])
    kernel = jnp.einsum("mlc,mc->lc", powers, residue * mode_gain, precision=HIGH)
    distance = jnp.arange(block_len)[:, None] - jnp.arange(block_len)[None, :]
    toeplitz = jnp.where(
        (distance >= 0)[:, :, None], kernel[jnp.maximum(distance, 0)], jnp.float32(0.0)
    )
    closing = (
        jnp.exp(-decay_rate[:, None, :] * (block_len - 1.0 - offsets)[None, :, None])
        * mode_gain[:, None, :]
    )
    opening = residue[:, None, :] * jnp.exp(
        -decay_rate[:, None, :] * (offsets + 1.0)[None, :, None]
    )
    return (toeplitz, closing, opening)


def block_pass(mixed, decay_rate, residue):
    block_len = 32
    toeplitz, closing, opening = block_tables(decay_rate, residue, block_len)
    blocked = mixed.reshape(-1, block_len, mixed.shape[1])
    inner = jnp.einsum("tsc,bsc->btc", toeplitz, blocked, precision=HIGH)
    block_ends = jnp.einsum("msc,bsc->bmc", closing, blocked, precision=HIGH)
    step_decay = jnp.broadcast_to(jnp.exp(-decay_rate * block_len), block_ends.shape)
    running = lax.associative_scan(combine, (step_decay, block_ends), axis=0)
    entering = jnp.concatenate([jnp.zeros_like(block_ends[:1]), running[1][:-1]], axis=0)
    return (blocked, inner, entering, opening, running[1][-1])


def local(query_rows, key_rows, value_rows, short_filter, decay_rate, residue, bypass):
    edge_rows = jnp.stack([query_rows[-2:], key_rows[-2:], value_rows[-2:]])
    before = shifted(edge_rows, "ctx", 1)
    query_feat = featurize(query_rows, short_filter[0], before[0])
    key_feat = featurize(key_rows, short_filter[1], before[1])
    value_feat = featurize(value_rows, short_filter[2], before[2])
    gated = key_feat * value_feat
    blocked, inner, entering, opening, device_end = block_pass(gated, decay_rate, residue)
    device_decay = jnp.exp(-decay_rate * gated.shape[0])

    def relay(position, incoming):
        return shifted(device_decay * incoming + device_end, "ctx", 1)

    arriving = lax.fori_loop(0, lax.axis_size("ctx") - 1, relay, jnp.zeros_like(device_end))
    block_starts = jnp.arange(blocked.shape[0]).astype(jnp.float32) * blocked.shape[1]
    entering = entering + jnp.exp(-decay_rate[None] * block_starts[:, None, None]) * arriving[None]
    total = inner + jnp.einsum("mtc,bmc->btc", opening, entering, precision=HIGH) + bypass * blocked
    return (query_feat * total.reshape(gated.shape)).astype(jnp.bfloat16)


def solution(mesh):
    placed = (
        P(("parts", "ctx"), ("chan", "sub")),
        P(("parts", "ctx"), ("chan", "sub")),
        P(("parts", "ctx"), ("chan", "sub")),
        P(None, None, ("chan", "sub")),
        P(None, ("chan", "sub")),
        P(None, ("chan", "sub")),
        P(("chan", "sub")),
    )
    return jax.shard_map(
        local,
        mesh=mesh,
        in_specs=placed,
        out_specs=P(("parts", "ctx"), ("chan", "sub")),
        check_vma=False,
    )
```

profile of v0, /device:TPU:24, one launch (start us, length us, event | category | flops | bytes accessed | tf_op | source)
XLA Modules:
  0.0 225.4 jit_solution(6520711272594571138)
XLA Ops:
  0.0 0.8 slice_bitcast_fusion.5
  0.8 0.8 slice_bitcast_fusion.3
  1.6 0.6 pad_maximum_fusion.1
  2.3 1.3 collective-permute-start.1
  3.5 0.5 broadcast_subtract_fusion
  4.0 0.6 convert_multiply_fusion
  4.6 0.5 iota_convert_fusion
  5.2 1.7 fusion.32
  6.8 1.8 multiply_exponential_fusion
  8.6 0.3 copy.66
  8.9 0.3 copy.82
  9.3 0.1 reshape.82
  9.3 12.3 %multiply_reduce_fusion = f32[2048,32]{1,0:T(8,128)S(1)} fusion(f32[2048,16]{1,0:T(8,128)S(1)} %copy.82, f32[32]{0:T(128)} %iota_convert_fusion, f32[16,2048]{0,1:T(8,128)S(1)} %copy.66), kind=kLoop, calls=%fused_computation.4 | loop fusion | flops 3080192 | bytes 524416
  21.7 0.5 broadcast_add_fusion
  22.2 1.3 copy.72
  23.6 2.2 copy.69
  25.8 0.3 copy.81
  26.1 6.8 %gather_fusion = f32[1024,2048]{1,0:T(8,128)} fusion(f32[32,2048]{1,0:T(8,128)S(1)} %bitcast.47, s32[1024]{0:T(1024)S(1)} %broadcast_clamp_fusion), kind=kCustom, calls=%fused_computation | custom fusion | bytes 16781312 | tf_op jit(solution)/shard_map/gather | solution.py:32
  33.0 26.4 %copy.67 = f32[32,32,2048]{1,0,2:T(8,128)} copy(f32[32,32,2048]{2,1,0:T(8,128)} %bitcast.48) | data formatting | bytes 16777216 | tf_op jit(solution)/shard_map/gather | solution.py:32
  59.4 0.0 collective-permute-done.1
  59.4 1.3 slice_bitcast_fusion.1
  60.7 0.1 maximum_convert_fusion.1
  60.9 0.1 maximum_convert_fusion.2
  61.1 0.7 fusion.19
  61.8 3.1 %copy.68 = f32[4,32,2048]{1,0,2:T(4,128)} copy(f32[4,32,2048]{2,1,0:T(8,128)S(1)} %bitcast.49) | data formatting | bytes 2097152 | tf_op jit(solution)/shard_map/reshape | solution.py:47
  64.9 34.5 %fusion.6 = f32[2048,4,16]{2,1,0:T(4,128)} fusion(f32[4,32,2048]{1,0,2:T(4,128)} %copy.68, f32[16,2048]{0,1:T(8,128)S(1)} %copy-done.1, f32[32]{0:T(128)S(1)} %copy-done.18, f32[16,2048]{0,1:T(8,128)S(1)} %copy.66), kind=kOutput, calls=%fused_computation.9 | convolution fusion | flops 52428800 | bytes 1835136 | tf_op jit(solution)/shard_map/msc,bsc->bmc/dot_general | solution.py:49
  99.4 3.5 %copy.71 = f32[2048,4,16]{0,2,1:T(8,128)S(1)} copy(f32[2048,4,16]{2,1,0:T(4,128)} %fusion.6) | data formatting | bytes 1048576 | tf_op jit(solution)/shard_map/msc,bsc->bmc/dot_general | solution.py:49
  103.1 0.1 pad.17
  103.2 1.5 pad.57
  104.6 1.5 pad.16
  106.1 0.9 add_bitcast_fusion
  107.1 1.8 slice_add_fusion
  108.9 21.6 %while.10 = (s32[]{:T(128)}, f32[16,2048]{1,0:T(8,128)S(1)}, f32[16,2048]{1,0:T(8,128)S(1)}, f32[16,2048]{1,0:T(8,128)S(1)}, s32[]{:T(128)}) while((s32[]{:T(128)}, f32[16,2048]{1,0:T(8,128)S(1)}, f32[16,2048]{1,0:T(8,128)S(1)}, f32[16,2048]{1,0:T(8,128)S(1)}, s32[]{:T(128)}) %tuple.39), condition=%wide.region_1.2_spmd, body=%wide.region_0.1_spmd.sunk | while | flops 65538 | bytes 1048677 | solution.py:69
  108.9 1.3 collective-permute-start
  110.2 6.5 %collective-permute-done = f32[16,2048]{1,0:T(8,128)S(1)} collective-permute-done((f32[16,2048]{1,0:T(8,128)S(1)}, f32[16,2048]{1,0:T(8,128)S(1)}, u32[]{:S(2)}, u32[]{:S(2)}) %collective-permute-start) | collective-permute-done | bytes 131104 | tf_op jit(solution)/shard_map/while/body/eval_jaxpr/ppermute | solution.py:12
  116.7 1.3 collective-permute-start
  118.0 5.6 %collective-permute-done = f32[16,2048]{1,0:T(8,128)S(1)} collective-permute-done((f32[16,2048]{1,0:T(8,128)S(1)}, f32[16,2048]{1,0:T(8,128)S(1)}, u32[]{:S(2)}, u32[]{:S(2)}) %collective-permute-start) | collective-permute-done | bytes 131104 | tf_op jit(solution)/shard_map/while/body/eval_jaxpr/ppermute | solution.py:12
  123.6 1.3 collective-permute-start
  124.9 5.6 %collective-permute-done = f32[16,2048]{1,0:T(8,128)S(1)} collective-permute-done((f32[16,2048]{1,0:T(8,128)S(1)}, f32[16,2048]{1,0:T(8,128)S(1)}, u32[]{:S(2)}, u32[]{:S(2)}) %collective-permute-start) | collective-permute-done | bytes 131104 | tf_op jit(solution)/shard_map/while/body/eval_jaxpr/ppermute | solution.py:12
  130.5 1.2 multiply_add_fusion.1
  131.6 3.1 %copy.73 = f32[4,16,2048]{1,0,2:T(4,128)} copy(f32[4,16,2048]{2,1,0:T(8,128)S(1)} %multiply_add_fusion.1) | data formatting | bytes 1048576 | tf_op jit(solution)/shard_map/add | solution.py:71
  134.7 24.1 %fusion.2 = f32[2048,4,32]{2,1,0:T(4,128)} fusion(f32[4,16,2048]{1,0,2:T(4,128)} %copy.73, f32[32]{0:T(128)S(1)} %copy-done.17, f32[16,2048]{0,1:T(8,128)} %copy.72, f32[16,2048]{0,1:T(8,128)S(1)} %copy.66), kind=kOutput, calls=%fused_computation.5 | convolution fusion | flops 52428800 | bytes 1835136 | tf_op jit(solution)/shard_map/mtc,bmc->btc/dot_general | solution.py:72
  158.8 3.5 %copy.75 = f32[2048,4,32]{0,2,1:T(8,128)S(1)} copy(f32[2048,4,32]{2,1,0:T(4,128)} %fusion.2) | data formatting | bytes 2097152 | tf_op jit(solution)/shard_map/mtc,bmc->btc/dot_general | solution.py:72
  162.3 57.0 %fusion = f32[2048,4,32]{2,1,0:T(4,128)} fusion(f32[4,32,2048]{1,0,2:T(4,128)} %copy.68, f32[32,32,2048]{1,0,2:T(8,128)} %copy.67, pred[32,32]{1,0:T(8,128)(4,1)S(1)} %subtract_compare_fusion), kind=kOutput, calls=%fused_computation.2 | convolution fusion | flops 102760448 | bytes 10486784 | tf_op jit(solution)/shard_map/tsc,bsc->btc/dot_general | solution.py:48
  219.3 3.5 %copy.74 = f32[2048,4,32]{0,2,1:T(8,128)S(1)} copy(f32[2048,4,32]{2,1,0:T(4,128)} %fusion) | data formatting | bytes 2097152 | tf_op jit(solution)/shard_map/tsc,bsc->btc/dot_general | solution.py:48
  222.8 1.2 maximum_convert_fusion
  224.0 0.2 bitcast_add_fusion
  224.2 1.2 fusion.25
  (50 shorter events, 0.3 us)
Async XLA Ops:
  0.0 22.2 %copy-start.4 = (f32[16,2048]{1,0:T(8,128)S(1)}, f32[16,2048]{1,0:T(8,128)}, u32[]{:S(2)}) copy-start(f32[16,2048]{1,0:T(8,128)} %param.14) | copy-start | bytes 393220
  2.3 57.1 %collective-permute-start.1 = (bf16[3,2,2048]{2,1,0:T(2,128)(2,1)}, bf16[3,2,2048]{2,1,0:T(2,128)(2,1)}, u32[]{:S(2)}, u32[]{:S(2)}) collective-permute-start(bf16[3,2,2048]{2,1,0:T(2,128)(2,1)} %pad_maximum_fusion.1), channel_id=1, source_target_pairs={{0,4},{4,8},{8,12},{1,5},{5,9},{9,13},{2,6},{6,10},{10,14},{3,7},{... | collective-permute-start | bytes 73736 | tf_op jit(solution)/shard_map/ppermute | solution.py:12
  32.9 27.8 %copy-start.2 = (bf16[128,2048]{1,0:T(8,128)(2,1)S(1)}, bf16[128,2048]{1,0:T(8,128)(2,1)}, u32[]{:S(2)}) copy-start(bf16[128,2048]{1,0:T(8,128)(2,1)} %param.10) | copy-start | bytes 1572868
  32.9 28.0 %copy-start.3 = (bf16[128,2048]{1,0:T(8,128)(2,1)S(1)}, bf16[128,2048]{1,0:T(8,128)(2,1)}, u32[]{:S(2)}) copy-start(bf16[128,2048]{1,0:T(8,128)(2,1)} %param.11) | copy-start | bytes 1572868
  32.9 28.1 %copy-start.8 = (f32[1,1,2048]{2,1,0:T(1,128)S(1)}, f32[1,1,2048]{2,1,0:T(1,128)}, u32[]{:S(2)}) copy-start(f32[1,1,2048]{2,1,0:T(1,128)} %get-tuple-element.62) | copy-start | bytes 24580
  32.9 28.1 %copy-start.9 = (f32[1,1,2048]{2,1,0:T(1,128)S(1)}, f32[1,1,2048]{2,1,0:T(1,128)}, u32[]{:S(2)}) copy-start(f32[1,1,2048]{2,1,0:T(1,128)} %get-tuple-element.63) | copy-start | bytes 24580
  32.9 28.1 %copy-start.10 = (f32[1,1,2048]{2,1,0:T(1,128)S(1)}, f32[1,1,2048]{2,1,0:T(1,128)}, u32[]{:S(2)}) copy-start(f32[1,1,2048]{2,1,0:T(1,128)} %get-tuple-element.64) | copy-start | bytes 24580
  32.9 28.1 %copy-start.11 = (f32[1,1,2048]{2,1,0:T(1,128)S(1)}, f32[1,1,2048]{2,1,0:T(1,128)}, u32[]{:S(2)}) copy-start(f32[1,1,2048]{2,1,0:T(1,128)} %get-tuple-element.65) | copy-start | bytes 24580
  32.9 28.1 %copy-start.12 = (f32[1,1,2048]{2,1,0:T(1,128)S(1)}, f32[1,1,2048]{2,1,0:T(1,128)}, u32[]{:S(2)}) copy-start(f32[1,1,2048]{2,1,0:T(1,128)} %get-tuple-element.68) | copy-start | bytes 24580
  32.9 28.1 %copy-start.13 = (f32[1,1,2048]{2,1,0:T(1,128)S(1)}, f32[1,1,2048]{2,1,0:T(1,128)}, u32[]{:S(2)}) copy-start(f32[1,1,2048]{2,1,0:T(1,128)} %get-tuple-element.69) | copy-start | bytes 24580
  61.8 3.2 %copy-start.1 = (f32[16,2048]{0,1:T(8,128)S(1)}, f32[16,2048]{0,1:T(8,128)}, u32[]{:S(2)}) copy-start(f32[16,2048]{0,1:T(8,128)} %copy.69) | copy-start | bytes 393220
  61.8 3.2 %copy-start.18 = (f32[32]{0:T(128)S(1)}, f32[32]{0:T(128)}, u32[]{:S(2)}) copy-start(f32[32]{0:T(128)} %broadcast_subtract_fusion) | copy-start | bytes 388
  99.4 3.5 %copy-start.5 = (f32[16,2048]{1,0:T(8,128)S(1)}, f32[16,2048]{1,0:T(8,128)}, u32[]{:S(2)}) copy-start(f32[16,2048]{1,0:T(8,128)} %get-tuple-element.58) | copy-start | bytes 393220
  99.4 3.5 %copy-start = (f32[16,2048]{1,0:T(8,128)S(1)}, f32[16,2048]{1,0:T(8,128)}, u32[]{:S(2)}) copy-start(f32[16,2048]{1,0:T(8,128)} %param.13) | copy-start | bytes 393220
  103.0 27.5 %copy-start.16 = (f32[4]{0:T(128)S(1)}, f32[4]{0:T(128)}, u32[]{:S(2)}) copy-start(f32[4]{0:T(128)} %convert_multiply_fusion) | copy-start | bytes 52
  108.9 25.9 %copy-start.17 = (f32[32]{0:T(128)S(1)}, f32[32]{0:T(128)}, u32[]{:S(2)}) copy-start(f32[32]{0:T(128)} %broadcast_add_fusion) | copy-start | bytes 388
  108.9 7.8 %collective-permute-start = (f32[16,2048]{1,0:T(8,128)S(1)}, f32[16,2048]{1,0:T(8,128)S(1)}, u32[]{:S(2)}, u32[]{:S(2)}) collective-permute-start(f32[16,2048]{1,0:T(8,128)S(1)} %multiply_add_fusion.3), channel_id=1, source_target_pairs={{0,4},{4,8},{8,12},{1,5},{5,9},{9,13},{2,6},{6,10},{10,14},{3,7},{... | collective-permute-start | bytes 393224 | tf_op jit(solution)/shard_map/while/body/eval_jaxpr/ppermute | solution.py:12
  116.7 6.9 %collective-permute-start = (f32[16,2048]{1,0:T(8,128)S(1)}, f32[16,2048]{1,0:T(8,128)S(1)}, u32[]{:S(2)}, u32[]{:S(2)}) collective-permute-start(f32[16,2048]{1,0:T(8,128)S(1)} %multiply_add_fusion.3), channel_id=1, source_target_pairs={{0,4},{4,8},{8,12},{1,5},{5,9},{9,13},{2,6},{6,10},{10,14},{3,7},{... | collective-permute-start | bytes 393224 | tf_op jit(solution)/shard_map/while/body/eval_jaxpr/ppermute | solution.py:12
  123.6 6.9 %collective-permute-start = (f32[16,2048]{1,0:T(8,128)S(1)}, f32[16,2048]{1,0:T(8,128)S(1)}, u32[]{:S(2)}, u32[]{:S(2)}) collective-permute-start(f32[16,2048]{1,0:T(8,128)S(1)} %multiply_add_fusion.3), channel_id=1, source_target_pairs={{0,4},{4,8},{8,12},{1,5},{5,9},{9,13},{2,6},{6,10},{10,14},{3,7},{... | collective-permute-start | bytes 393224 | tf_op jit(solution)/shard_map/while/body/eval_jaxpr/ppermute | solution.py:12
  219.3 3.5 %copy-start.14 = (bf16[2,2048]{1,0:T(2,128)(2,1)S(1)}, bf16[2,2048]{1,0:T(2,128)(2,1)}, u32[]{:S(2)}) copy-start(bf16[2,2048]{1,0:T(2,128)(2,1)} %get-tuple-element.72) | copy-start | bytes 24580
  219.3 4.7 %copy-start.15 = (f32[2048]{0:T(1024)S(1)}, f32[2048]{0:T(1024)}, u32[]{:S(2)}) copy-start(f32[2048]{0:T(1024)} %param.15) | copy-start | bytes 24580
  222.8 1.5 copy-start.6
  222.8 1.5 copy-start.7
where the time goes:
time: 228 us; the launch traced here: 225 us
  matrix products  116 us (51%)
  local copies, waits for them, and re-layouts  62.2 us (27%)
  other arithmetic  24.5 us (11%)
  waiting for transfers between devices  17.6 us (8%)
  starting transfers between devices  5.16 us (2%)
    dot_general x1, matrix products, block_pass(): inner = jnp.einsum('tsc,bsc->btc', toeplitz, blocked, precision=HIGH)  57 us
    dot_general x1, matrix products, block_pass(): block_ends = jnp.einsum('msc,bsc->bmc', closing, blocked, precision=HIGH)  34.5 us
    gather x2, local copies, waits for them, and re-layouts, block_tables(): kernel[jnp.maximum(distance, 0)]  33.2 us
    dot_general x1, matrix products, local(): jnp.einsum('mtc,bmc->btc', opening, entering, precision=HIGH)  24.1 us
    ppermute x4, waiting for transfers between devices, shifted(): lax.ppermute(value, axis, [(source, source + steps) for source in range(l...  17.6 us
    unnamed x1, other arithmetic  12.3 us
    ppermute x4, starting transfers between devices, shifted(): lax.ppermute(value, axis, [(source, source + steps) for source in range(l...  5.16 us
  transfers between devices with their start and end apart: 4, of which 3 were waited for; matrix products, arithmetic and copies ran while one was open for 25% of the time, Pallas kernels for 0%

commit v1 on v0

v1 whole, which is shorter than its diff:
```python
import functools

import jax
import jax.numpy as jnp
from jax import lax
from jax.experimental import pallas as pl
from jax.experimental.pallas import tpu as pltpu
from jax.sharding import PartitionSpec as P

MESH = pl.DeviceIdType.MESH
SEG = 8
LANES = 128


def kernel(
    n,
    chunks,
    q_ref,
    k_ref,
    v_ref,
    taps_ref,
    decay_ref,
    residue_ref,
    bypass_ref,
    out_ref,
    halo_out,
    halo_in,
    halo,
    stage,
    gated,
    query,
    total,
    local_p,
    arrive_p,
    powers,
    gains,
    seg_decay,
    ends,
    outgoing,
    incoming,
    halo_send,
    halo_recv,
    state_send,
    state_recv,
):
    z = lax.axis_index("ctx")
    tokens, channels = q_ref.shape
    modes = decay_ref.shape[0]
    length = tokens // SEG
    half = channels // 2
    width = channels // chunks
    groups = width // LANES
    has_left = z > 0
    has_right = z < n - 1

    barrier = pltpu.get_barrier_semaphore()

    @pl.when(has_left)
    def _():
        pl.semaphore_signal(barrier, inc=1, device_id={"ctx": z - 1}, device_id_type=MESH)

    @pl.when(has_right)
    def _():
        pl.semaphore_signal(barrier, inc=1, device_id={"ctx": z + 1}, device_id_type=MESH)

    tails = [ref[tokens - 16 :, :].astype(jnp.float32)[14:16] for ref in (q_ref, k_ref, v_ref)]
    rows = jnp.concatenate(tails + [jnp.zeros((2, channels), jnp.float32)], axis=0)
    halo_out[...] = jnp.concatenate([rows[:, :half], rows[:, half:]], axis=0).astype(jnp.bfloat16)

    @pl.when(jnp.logical_and(has_left, has_right))
    def _():
        pl.semaphore_wait(barrier, 2)

    @pl.when(has_left != has_right)
    def _():
        pl.semaphore_wait(barrier, 1)

    def halo_copy():
        return pltpu.make_async_remote_copy(
            src_ref=halo_out,
            dst_ref=halo_in,
            send_sem=halo_send,
            recv_sem=halo_recv,
            device_id={"ctx": z + 1},
            device_id_type=MESH,
        )

    def state_copy(chunk):
        return pltpu.make_async_remote_copy(
            src_ref=outgoing.at[chunk],
            dst_ref=incoming.at[chunk],
            send_sem=state_send.at[chunk],
            recv_sem=state_recv.at[chunk],
            device_id={"ctx": z + 1},
            device_id_type=MESH,
        )

    @pl.when(has_right)
    def _():
        halo_copy().start()

    decay = decay_ref[...]
    powers[...] = jnp.exp(-decay)
    gains[...] = residue_ref[...] * jnp.sqrt(one_minus_exp(2.0 * decay))
    for level in range(3):
        seg_decay[level] = jnp.exp(decay * (-1.0 * length * 2**level))

    @pl.when(jnp.logical_not(has_left))
    def _():
        halo[...] = jnp.zeros_like(halo)
        incoming[...] = jnp.zeros_like(incoming)

    @pl.when(has_left)
    def _():
        halo_copy().wait_recv()
        landed = halo_in[...].astype(jnp.float32)
        halo[:, :half] = landed[:8]
        halo[:, half:] = landed[8:]

    segment = lax.broadcasted_iota(jnp.int32, (SEG, LANES), 0)

    def spread(row):
        return jnp.broadcast_to(row, (SEG, LANES))

    def delayed(value, steps):
        return jnp.where(segment >= steps, pltpu.roll(value, steps, 0), 0.0)

    def featurized(ref, which, slot, lanes):
        stage[slot] = ref[:, lanes].astype(jnp.float32)
        parts = [stage[slot, pl.ds(b, SEG, stride=length), :] for b in range(length)]
        edge = halo[:, lanes]
        first = segment == 0
        before = [
            jnp.where(first, spread(edge[2 * which + r : 2 * which + r + 1]), pltpu.roll(parts[length - 2 + r], 1, 0))
            for r in range(2)
        ]
        joined = before + parts
        taps = [spread(taps_ref[which, i : i + 1, lanes]) for i in range(3)]
        return [taps[0] * joined[b + 2] + taps[1] * joined[b + 1] + taps[2] * joined[b] for b in range(length)]

    def columns(chunk, group):
        return pl.ds(pl.multiple_of(chunk * width + group * LANES, LANES), LANES)

    def inside(group):
        return pl.ds(pl.multiple_of(group * LANES, LANES), LANES)

    def close_chunk(chunk, carry):
        def close_group(group, carry):
            lanes = columns(chunk, group)
            keys = featurized(k_ref, 1, 0, lanes)
            values = featurized(v_ref, 2, 1, lanes)
            signal = [keys[b] * values[b] for b in range(length)]
            for b in range(length):
                gated[b * SEG : (b + 1) * SEG, lanes] = signal[b]
            base = [spread(powers[m : m + 1, lanes]) for m in range(modes)]
            state = [signal[0]] * modes
            for b in range(1, length):
                state = [base[m] * state[m] + signal[b] for m in range(modes)]
            for m in range(modes):
                scan = state[m]
                for level in range(3):
                    scan = scan + spread(seg_decay[level, m : m + 1, lanes]) * delayed(scan, 2**level)
                ends[chunk, m : m + 1, inside(group)] = scan[SEG - 1 :]
                local_p[m * SEG : (m + 1) * SEG, lanes] = spread(gains[m : m + 1, lanes]) * delayed(scan, 1)
            return carry

        lax.fori_loop(0, groups, close_group, 0)

        @pl.when(jnp.logical_and(jnp.logical_not(has_left), has_right))
        def _():
            outgoing[chunk] = ends[chunk]
            state_copy(chunk).start()

        return carry

    lax.fori_loop(0, chunks, close_chunk, 0)

    def relay_chunk(chunk, carry):
        @pl.when(jnp.logical_and(has_left, has_right))
        def _():
            span = pl.ds(pl.multiple_of(chunk * width, LANES), width)
            step = jnp.exp(decay_ref[:, span] * (-1.0 * tokens))
            state_copy(chunk).wait_recv()
            outgoing[chunk] = step * incoming[chunk] + ends[chunk]
            state_copy(chunk).start()

        def local_group(group, carry):
            lanes = columns(chunk, group)
            base = powers[:, lanes]
            term = gains[:, lanes]
            taps = []
            for lag in range(length):
                row = jnp.sum(term, axis=0, keepdims=True)
                if lag == 0:
                    row = row + bypass_ref[:, lanes]
                taps.append(spread(row))
                term = term * base
            signal = [gated[b * SEG : (b + 1) * SEG, lanes] for b in range(length)]
            for b in range(length):
                acc = taps[0] * signal[b]
                for lag in range(1, b + 1):
                    acc = acc + taps[lag] * signal[b - lag]
                total[b * SEG : (b + 1) * SEG, lanes] = acc
            feat = featurized(q_ref, 0, 0, lanes)
            for b in range(length):
                query[b * SEG : (b + 1) * SEG, lanes] = feat[b]
            distance = segment.astype(jnp.float32) * (-1.0 * length)
            for m in range(modes):
                arrive_p[m * SEG : (m + 1) * SEG, lanes] = spread(gains[m : m + 1, lanes]) * jnp.exp(
                    spread(decay_ref[m : m + 1, lanes]) * distance
                )
            return carry

        lax.fori_loop(0, groups, local_group, 0)
        return carry

    lax.fori_loop(0, chunks, relay_chunk, 0)

    def open_chunk(chunk, carry):
        @pl.when(jnp.logical_and(has_left, jnp.logical_not(has_right)))
        def _():
            state_copy(chunk).wait_recv()

        def open_group(group, carry):
            lanes = columns(chunk, group)
            base = [spread(powers[m : m + 1, lanes]) for m in range(modes)]
            term = [
                local_p[m * SEG : (m + 1) * SEG, lanes]
                + arrive_p[m * SEG : (m + 1) * SEG, lanes] * spread(incoming[chunk, m : m + 1, inside(group)])
                for m in range(modes)
            ]
            for b in range(length):
                term = [term[m] * base[m] for m in range(modes)]
                sums = term
                while len(sums) > 1:
                    sums = [x + y for x, y in zip(sums[::2], sums[1::2])] + sums[len(sums) & ~1 :]
                rows = slice(b * SEG, (b + 1) * SEG)
                stage[0, pl.ds(b, SEG, stride=length), :] = query[rows, lanes] * (total[rows, lanes] + sums[0])
            out_ref[:, lanes] = stage[0].astype(jnp.bfloat16)
            return carry

        lax.fori_loop(0, groups, open_group, 0)
        return carry

    lax.fori_loop(0, chunks, open_chunk, 0)

    @pl.when(has_right)
    def _():
        halo_copy().wait_send()

        def drain(chunk, carry):
            state_copy(chunk).wait_send()
            return carry

        lax.fori_loop(0, chunks, drain, 0)


def one_minus_exp(x):
    series = jnp.ones_like(x)
    for order in range(10, 1, -1):
        series = 1.0 - series * x * (1.0 / order)
    return jnp.where(x < 0.5, x * series, 1.0 - jnp.exp(-x))


def local(query_rows, key_rows, value_rows, short_filter, decay_rate, residue, bypass):
    tokens, channels = query_rows.shape
    modes = decay_rate.shape[0]
    chunks = 4
    n = lax.axis_size("ctx")
    length = tokens // SEG
    width = channels // chunks
    f32 = jnp.float32
    return pl.pallas_call(
        functools.partial(kernel, n, chunks),
        out_shape=jax.ShapeDtypeStruct((tokens, channels), jnp.bfloat16),
        in_specs=[pl.BlockSpec(memory_space=pltpu.VMEM)] * 7,
        out_specs=pl.BlockSpec(memory_space=pltpu.VMEM),
        scratch_shapes=[
            pltpu.VMEM((16, channels // 2), jnp.bfloat16),
            pltpu.VMEM((16, channels // 2), jnp.bfloat16),
            pltpu.VMEM((8, channels), f32),
            pltpu.VMEM((2, tokens, LANES), f32),
            pltpu.VMEM((tokens, channels), f32),
            pltpu.VMEM((tokens, channels), f32),
            pltpu.VMEM((tokens, channels), f32),
            pltpu.VMEM((modes * SEG, channels), f32),
            pltpu.VMEM((modes * SEG, channels), f32),
            pltpu.VMEM((modes, channels), f32),
            pltpu.VMEM((modes, channels), f32),
            pltpu.VMEM((3, modes, channels), f32),
            pltpu.VMEM((chunks, modes, width), f32),
            pltpu.VMEM((chunks, modes, width), f32),
            pltpu.VMEM((chunks, modes, width), f32),
            pltpu.SemaphoreType.DMA,
            pltpu.SemaphoreType.DMA,
            pltpu.SemaphoreType.DMA((chunks,)),
            pltpu.SemaphoreType.DMA((chunks,)),
        ],
        compiler_params=pltpu.CompilerParams(
            collective_id=0, has_side_effects=True, vmem_limit_bytes=32 * 1024 * 1024
        ),
        cost_estimate=pl.CostEstimate(
            flops=100 * tokens * channels, bytes_accessed=8 * tokens * channels, transcendentals=0
        ),
    )(query_rows, key_rows, value_rows, short_filter, decay_rate, residue, bypass[None, :])


def solution(mesh):
    placed = (
        P(("parts", "ctx"), ("chan", "sub")),
        P(("parts", "ctx"), ("chan", "sub")),
        P(("parts", "ctx"), ("chan", "sub")),
        P(None, None, ("chan", "sub")),
        P(None, ("chan", "sub")),
        P(None, ("chan", "sub")),
        P(("chan", "sub")),
    )
    return jax.shard_map(
        local,
        mesh=mesh,
        in_specs=placed,
        out_specs=P(("parts", "ctx"), ("chan", "sub")),
        check_vma=False,
    )
```

time: 228 us -> 21 us (0.09); the launches traced: 225 us -> 20.7 us
  matrix products: 116 us -> 0 us
  local copies, waits for them, and re-layouts: 62.2 us -> 7.31 us
  other arithmetic: 24.5 us -> 0 us
  waiting for transfers between devices: 17.6 us -> 0 us
  Pallas kernels: 0 us -> 13.4 us
  starting transfers between devices: 5.16 us -> 0 us
    dot_general x3 -> x0, matrix products: 116 us -> none  [the longest x1 57 us: block_pass(): inner = jnp.einsum('tsc,bsc->btc', toeplitz, blocked, precision=HIGH)]
    gather x2 -> x0, local copies, waits for them, and re-layouts: 33.2 us -> none  [block_tables(): kernel[jnp.maximum(distance, 0)]]
    ppermute x4 -> x0, waiting for transfers between devices: 17.6 us -> none  [shifted(): lax.ppermute(value, axis, [(source, source + steps) for source in range(l...]
    pallas_call x0 -> x1, Pallas kernels: none -> 13.4 us  [local(): pl.pallas_call(functools.partial(kernel, n, chunks), out_shape=jax.ShapeD...]
    unnamed x1 -> x0, other arithmetic: 12.3 us -> none
    dot_general x4 -> x0, local copies, waits for them, and re-layouts: 10.7 us -> none  [the longest x1 3.49 us: block_pass(): block_ends = jnp.einsum('msc,bsc->bmc', closing, blocked, precision=HIGH)]
    ppermute x4 -> x0, starting transfers between devices: 5.16 us -> none  [shifted(): lax.ppermute(value, axis, [(source, source + steps) for source in range(l...]
    unnamed x41 -> x15, local copies, waits for them, and re-layouts: 3.22 us -> 7.31 us
  transfers between devices with their start and end apart: 4 -> 0, of which waited for: 3 -> 0; matrix products, arithmetic and copies ran while one was open for 25% -> 0% of each run, Pallas kernels for 0% -> 0%
where the time goes in v1:
time: 21 us; the launch traced here: 20.7 us
  Pallas kernels  13.4 us (64%)
  local copies, waits for them, and re-layouts  7.31 us (35%)
    pallas_call x1, Pallas kernels, local(): pl.pallas_call(functools.partial(kernel, n, chunks), out_shape=jax.ShapeD...  13.4 us
    unnamed x15, local copies, waits for them, and re-layouts  7.31 us

profile of v1, /device:TPU:24, one launch (start us, length us, event | category | flops | bytes accessed | tf_op | source)
XLA Modules:
  0.0 20.7 jit_solution(7287495004219917436)
XLA Ops:
  0.0 0.0 copy-start
  0.0 1.0 %copy-done = bf16[128,2048]{1,0:T(8,128)(2,1)S(1)} copy-done((bf16[128,2048]{1,0:T(8,128)(2,1)S(1)}, bf16[128,2048]{1,0:T(8,128)(2,1)}, u32[]{:S(2)}) %copy-start) | copy-done | bytes 524312
  1.0 0.0 copy-start.1
  1.0 1.0 %copy-done.1 = bf16[128,2048]{1,0:T(8,128)(2,1)S(1)} copy-done((bf16[128,2048]{1,0:T(8,128)(2,1)S(1)}, bf16[128,2048]{1,0:T(8,128)(2,1)}, u32[]{:S(2)}) %copy-start.1) | copy-done | bytes 524312
  2.1 0.0 copy-start.2
  2.1 1.0 %copy-done.2 = bf16[128,2048]{1,0:T(8,128)(2,1)S(1)} copy-done((bf16[128,2048]{1,0:T(8,128)(2,1)S(1)}, bf16[128,2048]{1,0:T(8,128)(2,1)}, u32[]{:S(2)}) %copy-start.2) | copy-done | bytes 524312
  3.1 0.0 copy-start.3
  3.1 0.9 %copy-done.3 = f32[16,2048]{1,0:T(8,128)S(1)} copy-done((f32[16,2048]{1,0:T(8,128)S(1)}, f32[16,2048]{1,0:T(8,128)}, u32[]{:S(2)}) %copy-start.3) | copy-done | bytes 131096
  4.0 0.0 copy-start.4
  4.0 0.9 %copy-done.4 = f32[16,2048]{1,0:T(8,128)S(1)} copy-done((f32[16,2048]{1,0:T(8,128)S(1)}, f32[16,2048]{1,0:T(8,128)}, u32[]{:S(2)}) %copy-start.4) | copy-done | bytes 131096
  4.9 0.0 copy-start.5
  4.9 0.9 %copy-done.5 = f32[3,3,2048]{2,1,0:T(4,128)S(1)} copy-done((f32[3,3,2048]{2,1,0:T(4,128)S(1)}, f32[3,3,2048]{2,1,0:T(4,128)}, u32[]{:S(2)}) %copy-start.5) | copy-done | bytes 73752
  5.8 0.0 copy-start.6
  5.8 0.7 %copy-done.6 = f32[2048]{0:T(1024)S(1)} copy-done((f32[2048]{0:T(1024)S(1)}, f32[2048]{0:T(1024)}, u32[]{:S(2)}) %copy-start.6) | copy-done | bytes 8216
  6.5 13.4 %shard_map.73 = bf16[128,2048]{1,0:T(8,128)(2,1)S(1)} custom-call(bf16[128,2048]{1,0:T(8,128)(2,1)S(1)} %copy-done, bf16[128,2048]{1,0:T(8,128)(2,1)S(1)} %copy-done.1, bf16[128,2048]{1,0:T(8,128)(2,1)S(1)} %copy-done.2, f32[3,3,2048]{2,1,0:T(4,128)S(1)} %copy-done.5, f32[16,2048]{1,0:T(8,128)S(1)} %copy-done.3, f32[16,2048]{1,0:T(8,128)S(1)} %copy-done.4, ...), custom_call_target="tpu_custom_call" | custom-call | flops 26214400 | bytes 2097152 | tf_op jit(solution)/shard_map/pallas_call | solution.py:273
  19.9 0.8 %copy.9 = bf16[128,2048]{1,0:T(8,128)(2,1)} copy(bf16[128,2048]{1,0:T(8,128)(2,1)S(1)} %shard_map.73) | data formatting | bytes 1048576
Async XLA Ops:
  0.0 1.0 %copy-start = (bf16[128,2048]{1,0:T(8,128)(2,1)S(1)}, bf16[128,2048]{1,0:T(8,128)(2,1)}, u32[]{:S(2)}) copy-start(bf16[128,2048]{1,0:T(8,128)(2,1)} %q_ref.1) | copy-start | bytes 1572868
  1.0 1.0 %copy-start.1 = (bf16[128,2048]{1,0:T(8,128)(2,1)S(1)}, bf16[128,2048]{1,0:T(8,128)(2,1)}, u32[]{:S(2)}) copy-start(bf16[128,2048]{1,0:T(8,128)(2,1)} %k_ref.1) | copy-start | bytes 1572868
  2.1 1.0 %copy-start.2 = (bf16[128,2048]{1,0:T(8,128)(2,1)S(1)}, bf16[128,2048]{1,0:T(8,128)(2,1)}, u32[]{:S(2)}) copy-start(bf16[128,2048]{1,0:T(8,128)(2,1)} %v_ref.1) | copy-start | bytes 1572868
  3.1 0.9 %copy-start.3 = (f32[16,2048]{1,0:T(8,128)S(1)}, f32[16,2048]{1,0:T(8,128)}, u32[]{:S(2)}) copy-start(f32[16,2048]{1,0:T(8,128)} %decay_ref.1) | copy-start | bytes 393220
  4.0 0.9 %copy-start.4 = (f32[16,2048]{1,0:T(8,128)S(1)}, f32[16,2048]{1,0:T(8,128)}, u32[]{:S(2)}) copy-start(f32[16,2048]{1,0:T(8,128)} %residue_ref.1) | copy-start | bytes 393220
  4.9 0.9 %copy-start.5 = (f32[3,3,2048]{2,1,0:T(4,128)S(1)}, f32[3,3,2048]{2,1,0:T(4,128)}, u32[]{:S(2)}) copy-start(f32[3,3,2048]{2,1,0:T(4,128)} %taps_ref.1) | copy-start | bytes 221188
  5.8 0.7 %copy-start.6 = (f32[2048]{0:T(1024)S(1)}, f32[2048]{0:T(1024)}, u32[]{:S(2)}) copy-start(f32[2048]{0:T(1024)} %param.13) | copy-start | bytes 24580

commit v2 on v1

--- a/solution.py
+++ b/solution.py
@@ -15,6 +15,16 @@
 def kernel(
     n,
     chunks,
+    q_hbm,
+    k_hbm,
+    v_hbm,
+    taps_hbm,
+    decay_hbm,
+    residue_hbm,
+    bypass_hbm,
+    out_hbm,
+    out_ref,
+    stores,
     q_ref,
     k_ref,
     v_ref,
@@ -22,7 +32,9 @@
     decay_ref,
     residue_ref,
     bypass_ref,
-    out_ref,
+    loads,
+    firsts,
+    fix,
     halo_out,
     halo_in,
     halo,
@@ -44,8 +56,8 @@
     state_recv,
 ):
     z = lax.axis_index("ctx")
-    tokens, channels = q_ref.shape
-    modes = decay_ref.shape[0]
+    tokens, channels = q_hbm.shape
+    modes = decay_hbm.shape[0]
     length = tokens // SEG
     half = channels // 2
     width = channels // chunks
@@ -53,6 +65,16 @@
     has_left = z > 0
     has_right = z < n - 1
 
+    tail, body = pl.ds(tokens - 16, 16), pl.ds(0, tokens - 16)
+    signals = ((q_hbm, q_ref), (k_hbm, k_ref), (v_hbm, v_ref))
+    moves = [(src.at[tail], dst.at[tail]) for src, dst in signals]
+    moves += [(decay_hbm, decay_ref), (residue_hbm, residue_ref), (taps_hbm, taps_ref)]
+    moves += [(src.at[body], dst.at[body]) for src, dst in signals[1:] + signals[:1]]
+    moves += [(bypass_hbm, bypass_ref)]
+    copies = [pltpu.make_async_copy(src, dst, loads.at[i]) for i, (src, dst) in enumerate(moves)]
+    for copy in copies:
+        copy.start()
+
     barrier = pltpu.get_barrier_semaphore()
 
     @pl.when(has_left)
@@ -63,6 +85,8 @@
     def _():
         pl.semaphore_signal(barrier, inc=1, device_id={"ctx": z + 1}, device_id_type=MESH)
 
+    for copy in copies[:3]:
+        copy.wait()
     tails = [ref[tokens - 16 :, :].astype(jnp.float32)[14:16] for ref in (q_ref, k_ref, v_ref)]
     rows = jnp.concatenate(tails + [jnp.zeros((2, channels), jnp.float32)], axis=0)
     halo_out[...] = jnp.concatenate([rows[:, :half], rows[:, half:]], axis=0).astype(jnp.bfloat16)
@@ -85,6 +109,10 @@
             device_id_type=MESH,
         )
 
+    def store_copy(chunk):
+        span = pl.ds(pl.multiple_of(chunk * width, LANES), width)
+        return pltpu.make_async_copy(out_ref.at[:, span], out_hbm.at[:, span], stores.at[chunk])
+
     def state_copy(chunk):
         return pltpu.make_async_remote_copy(
             src_ref=outgoing.at[chunk],
@@ -99,23 +127,40 @@
     def _():
         halo_copy().start()
 
+    for copy in copies[3:6]:
+        copy.wait()
     decay = decay_ref[...]
     powers[...] = jnp.exp(-decay)
     gains[...] = residue_ref[...] * jnp.sqrt(one_minus_exp(2.0 * decay))
     for level in range(3):
         seg_decay[level] = jnp.exp(decay * (-1.0 * length * 2**level))
 
+    for copy in copies[6:8]:
+        copy.wait()
+
+    def first_tokens():
+        def pair(ref, which):
+            rows = ref[0:16, :].astype(jnp.float32)
+            now, after = rows[0:1], rows[1:2]
+            old, last = halo[2 * which : 2 * which + 1, :], halo[2 * which + 1 : 2 * which + 2, :]
+            t0, t1, t2 = [taps_ref[which, i : i + 1, :] for i in range(3)]
+            return t0 * now + t1 * last + t2 * old, t0 * after + t1 * now + t2 * last
+
+        keys, values = pair(k_ref, 1), pair(v_ref, 2)
+        first, second = keys[0] * values[0], keys[1] * values[1]
+        firsts[0:1, :] = first
+        firsts[1:2, :] = second
+        fix[...] = powers[...] * first + second
+
     @pl.when(jnp.logical_not(has_left))
     def _():
         halo[...] = jnp.zeros_like(halo)
         incoming[...] = jnp.zeros_like(incoming)
-
-    @pl.when(has_left)
-    def _():
-        halo_copy().wait_recv()
-        landed = halo_in[...].astype(jnp.float32)
-        halo[:, :half] = landed[:8]
-        halo[:, half:] = landed[8:]
+        first_tokens()
+
+    def closing(chunk):
+        span = pl.ds(pl.multiple_of(chunk * width, LANES), width)
+        return ends[chunk] + jnp.exp(decay_ref[:, span] * (2.0 - tokens)) * fix[:, span]
 
     segment = lax.broadcasted_iota(jnp.int32, (SEG, LANES), 0)
 
@@ -125,15 +170,13 @@
     def delayed(value, steps):
         return jnp.where(segment >= steps, pltpu.roll(value, steps, 0), 0.0)
 
-    def featurized(ref, which, slot, lanes):
+    def featurized(ref, which, slot, lanes, with_edge):
         stage[slot] = ref[:, lanes].astype(jnp.float32)
         parts = [stage[slot, pl.ds(b, SEG, stride=length), :] for b in range(length)]
-        edge = halo[:, lanes]
-        first = segment == 0
-        before = [
-            jnp.where(first, spread(edge[2 * which + r : 2 * which + r + 1]), pltpu.roll(parts[length - 2 + r], 1, 0))
-            for r in range(2)
-        ]
+        before = [pltpu.roll(parts[length - 2 + r], 1, 0) for r in range(2)]
+        if with_edge:
+            edge = [spread(halo[2 * which + r : 2 * which + r + 1, lanes]) for r in range(2)]
+            before = [jnp.where(segment == 0, e, x) for e, x in zip(edge, before)]
         joined = before + parts
         taps = [spread(taps_ref[which, i : i + 1, lanes]) for i in range(3)]
         return [taps[0] * joined[b + 2] + taps[1] * joined[b + 1] + taps[2] * joined[b] for b in range(length)]
@@ -147,9 +190,10 @@
     def close_chunk(chunk, carry):
         def close_group(group, carry):
             lanes = columns(chunk, group)
-            keys = featurized(k_ref, 1, 0, lanes)
-            values = featurized(v_ref, 2, 1, lanes)
+            keys = featurized(k_ref, 1, 0, lanes, False)
+            values = featurized(v_ref, 2, 1, lanes, False)
             signal = [keys[b] * values[b] for b in range(length)]
+            signal[:2] = [jnp.where(segment == 0, 0.0, value) for value in signal[:2]]
             for b in range(length):
                 gated[b * SEG : (b + 1) * SEG, lanes] = signal[b]
             base = [spread(powers[m : m + 1, lanes]) for m in range(modes)]
@@ -161,19 +205,30 @@
                 for level in range(3):
                     scan = scan + spread(seg_decay[level, m : m + 1, lanes]) * delayed(scan, 2**level)
                 ends[chunk, m : m + 1, inside(group)] = scan[SEG - 1 :]
-                local_p[m * SEG : (m + 1) * SEG, lanes] = spread(gains[m : m + 1, lanes]) * delayed(scan, 1)
+                local_p[m * SEG : (m + 1) * SEG, lanes] = scan
             return carry
 
         lax.fori_loop(0, groups, close_group, 0)
 
         @pl.when(jnp.logical_and(jnp.logical_not(has_left), has_right))
         def _():
-            outgoing[chunk] = ends[chunk]
+            outgoing[chunk] = closing(chunk)
             state_copy(chunk).start()
 
         return carry
 
     lax.fori_loop(0, chunks, close_chunk, 0)
+
+    @pl.when(has_left)
+    def _():
+        halo_copy().wait_recv()
+        landed = halo_in[...].astype(jnp.float32)
+        halo[:, :half] = landed[:8]
+        halo[:, half:] = landed[8:]
+        first_tokens()
+
+    for copy in copies[8:]:
+        copy.wait()
 
     def relay_chunk(chunk, carry):
         @pl.when(jnp.logical_and(has_left, has_right))
@@ -181,7 +236,7 @@
             span = pl.ds(pl.multiple_of(chunk * width, LANES), width)
             step = jnp.exp(decay_ref[:, span] * (-1.0 * tokens))
             state_copy(chunk).wait_recv()
-            outgoing[chunk] = step * incoming[chunk] + ends[chunk]
+            outgoing[chunk] = step * incoming[chunk] + closing(chunk)
             state_copy(chunk).start()
 
         def local_group(group, carry):
@@ -196,18 +251,25 @@
                 taps.append(spread(row))
                 term = term * base
             signal = [gated[b * SEG : (b + 1) * SEG, lanes] for b in range(length)]
+            signal[:2] = [jnp.where(segment == 0, spread(firsts[b : b + 1, lanes]), signal[b]) for b in range(2)]
             for b in range(length):
                 acc = taps[0] * signal[b]
                 for lag in range(1, b + 1):
                     acc = acc + taps[lag] * signal[b - lag]
                 total[b * SEG : (b + 1) * SEG, lanes] = acc
-            feat = featurized(q_ref, 0, 0, lanes)
+            feat = featurized(q_ref, 0, 0, lanes, True)
             for b in range(length):
                 query[b * SEG : (b + 1) * SEG, lanes] = feat[b]
             distance = segment.astype(jnp.float32) * (-1.0 * length)
+            lift = jnp.exp(2.0 * decay_ref[:, lanes]) * fix[:, lanes]
             for m in range(modes):
-                arrive_p[m * SEG : (m + 1) * SEG, lanes] = spread(gains[m : m + 1, lanes]) * jnp.exp(
-                    spread(decay_ref[m : m + 1, lanes]) * distance
+                rows = slice(m * SEG, (m + 1) * SEG)
+                gain = spread(gains[m : m + 1, lanes])
+                arrive = gain * jnp.exp(spread(decay_ref[m : m + 1, lanes]) * distance)
+                arrive_p[rows, lanes] = arrive
+                earlier = pltpu.roll(local_p[rows, lanes], 1, 0)
+                local_p[rows, lanes] = jnp.where(
+                    segment >= 1, gain * earlier + arrive * spread(lift[m : m + 1]), 0.0
                 )
             return carry
 
@@ -240,6 +302,7 @@
             return carry
 
         lax.fori_loop(0, groups, open_group, 0)
+        store_copy(chunk).start()
         return carry
 
     lax.fori_loop(0, chunks, open_chunk, 0)
@@ -253,6 +316,12 @@
             return carry
 
         lax.fori_loop(0, chunks, drain, 0)
+
+    def finish(chunk, carry):
+        store_copy(chunk).wait()
+        return carry
+
+    lax.fori_loop(0, chunks, finish, 0)
 
 
 def one_minus_exp(x):
@@ -265,7 +334,7 @@
 def local(query_rows, key_rows, value_rows, short_filter, decay_rate, residue, bypass):
     tokens, channels = query_rows.shape
     modes = decay_rate.shape[0]
-    chunks = 4
+    chunks = next(c for c in (8, 4, 2, 1) if channels % (c * LANES) == 0)
     n = lax.axis_size("ctx")
     length = tokens // SEG
     width = channels // chunks
@@ -273,9 +342,21 @@
     return pl.pallas_call(
         functools.partial(kernel, n, chunks),
         out_shape=jax.ShapeDtypeStruct((tokens, channels), jnp.bfloat16),
-        in_specs=[pl.BlockSpec(memory_space=pltpu.VMEM)] * 7,
-        out_specs=pl.BlockSpec(memory_space=pltpu.VMEM),
+        in_specs=[pl.BlockSpec(memory_space=pltpu.HBM)] * 7,
+        out_specs=pl.BlockSpec(memory_space=pltpu.HBM),
         scratch_shapes=[
+            pltpu.VMEM((tokens, channels), jnp.bfloat16),
+            pltpu.SemaphoreType.DMA((chunks,)),
+            pltpu.VMEM((tokens, channels), jnp.bfloat16),
+            pltpu.VMEM((tokens, channels), jnp.bfloat16),
+            pltpu.VMEM((tokens, channels), jnp.bfloat16),
+            pltpu.VMEM(short_filter.shape, f32),
+            pltpu.VMEM((modes, channels), f32),
+            pltpu.VMEM((modes, channels), f32),
+            pltpu.VMEM((1, channels), f32),
+            pltpu.SemaphoreType.DMA((10,)),
+            pltpu.VMEM((8, channels), f32),
+            pltpu.VMEM((modes, channels), f32),
             pltpu.VMEM((16, channels // 2), jnp.bfloat16),
             pltpu.VMEM((16, channels // 2), jnp.bfloat16),
             pltpu.VMEM((8, channels), f32),
@@ -297,7 +378,7 @@
             pltpu.SemaphoreType.DMA((chunks,)),
         ],
         compiler_params=pltpu.CompilerParams(
-            collective_id=0, has_side_effects=True, vmem_limit_bytes=32 * 1024 * 1024
+            collective_id=0, has_side_effects=True, vmem_limit_bytes=60 * 1024 * 1024
         ),
         cost_estimate=pl.CostEstimate(
             flops=100 * tokens * channels, bytes_accessed=8 * tokens * channels, transcendentals=0

time: 21 us -> 14.5 us (0.69)
  local copies, waits for them, and re-layouts: 7.31 us -> 1.88 us
  Pallas kernels: 13.4 us -> 12.4 us
    unnamed x15 -> x1, local copies, waits for them, and re-layouts: 7.31 us -> 1.88 us
    pallas_call x1, Pallas kernels: 13.4 us -> 12.4 us  [local(): pl.pallas_call(functools.partial(kernel, n, chunks), out_shape=jax.ShapeD...]
where the time goes in v2:
time: 14.5 us; the launch traced here: 14.3 us
  Pallas kernels  12.4 us (86%)
  local copies, waits for them, and re-layouts  1.88 us (13%)
    pallas_call x1, Pallas kernels, local(): pl.pallas_call(functools.partial(kernel, n, chunks), out_shape=jax.ShapeD...  12.4 us
    unnamed x1, local copies, waits for them, and re-layouts  1.88 us

profile of v2, /device:TPU:24, one launch (start us, length us, event | category | flops | bytes accessed | tf_op | source)
XLA Modules:
  0.0 14.3 jit_solution(17323719362922966173)
XLA Ops:
  0.0 12.4 %shard_map.73 = bf16[128,2048]{1,0:T(8,128)(2,1)} custom-call(bf16[128,2048]{1,0:T(8,128)(2,1)} %q_hbm.1, bf16[128,2048]{1,0:T(8,128)(2,1)} %k_hbm.1, bf16[128,2048]{1,0:T(8,128)(2,1)} %v_hbm.1, f32[3,3,2048]{2,1,0:T(4,128)} %taps_hbm.1, f32[16,2048]{1,0:T(8,128)} %decay_hbm.1, f32[16,2048]{1,0:T(8,128)} %residue_hbm.1, f32[1,2048]{1,0:T(1,128)} %bitcast.1), custom_call_target="tpu_custom_call" | custom-call | flops 26214400 | bytes 2097152 | tf_op jit(solution)/shard_map/pallas_call | solution.py:342
  12.4 1.9 %copy.9 = bf16[128,2048]{1,0:T(8,128)(2,1)} copy(bf16[128,2048]{1,0:T(8,128)(2,1)} %shard_map.73) | data formatting | bytes 1048576

commit v3 on v2

--- a/solution.py
+++ b/solution.py
@@ -334,7 +334,7 @@
 def local(query_rows, key_rows, value_rows, short_filter, decay_rate, residue, bypass):
     tokens, channels = query_rows.shape
     modes = decay_rate.shape[0]
-    chunks = next(c for c in (8, 4, 2, 1) if channels % (c * LANES) == 0)
+    chunks = next(c for c in (16, 8, 4, 2, 1) if channels % (c * LANES) == 0)
     n = lax.axis_size("ctx")
     length = tokens // SEG
     width = channels // chunks

time: 14.5 us -> 14.5 us (level)
  no operation moved by 1% of the time
where the time goes in v3:
time: 14.5 us; the launch traced here: 14.3 us
  Pallas kernels  12.5 us (86%)
  local copies, waits for them, and re-layouts  1.88 us (13%)
    pallas_call x1, Pallas kernels, local(): pl.pallas_call(functools.partial(kernel, n, chunks), out_shape=jax.ShapeD...  12.5 us
    unnamed x1, local copies, waits for them, and re-layouts  1.88 us

profile of v3, /device:TPU:24, one launch (start us, length us, event | category | flops | bytes accessed | tf_op | source)
XLA Modules:
  0.0 14.3 jit_solution(646571346613589666)
XLA Ops:
  0.0 12.5 %shard_map.73 = bf16[128,2048]{1,0:T(8,128)(2,1)} custom-call(bf16[128,2048]{1,0:T(8,128)(2,1)} %q_hbm.1, bf16[128,2048]{1,0:T(8,128)(2,1)} %k_hbm.1, bf16[128,2048]{1,0:T(8,128)(2,1)} %v_hbm.1, f32[3,3,2048]{2,1,0:T(4,128)} %taps_hbm.1, f32[16,2048]{1,0:T(8,128)} %decay_hbm.1, f32[16,2048]{1,0:T(8,128)} %residue_hbm.1, f32[1,2048]{1,0:T(1,128)} %bitcast.1), custom_call_target="tpu_custom_call" | custom-call | flops 26214400 | bytes 2097152 | tf_op jit(solution)/shard_map/pallas_call | solution.py:342
  12.5 1.9 %copy.9 = bf16[128,2048]{1,0:T(8,128)(2,1)} copy(bf16[128,2048]{1,0:T(8,128)(2,1)} %shard_map.73) | data formatting | bytes 1048576
